TPU v7x, 256 devices: a whole 4x4x8 slice. The times are simulated.
256 devices in a mesh: seq: 128 (over y_lo, x, z, core), ch: 2 (over y_hi).
Axes of the slice: x: 4, y: 4 (y_hi: 2, y_lo: 2; y = y_hi * 2 + y_lo), z: 8, core: 2. Of those that a mesh axis runs over, the one named last changes fastest.
Arguments:
- signal: bfloat16 [262144, 768], P('seq', 'ch'), may hold values from -6 to 6
- gate: bfloat16 [262144, 768], P('seq', 'ch'), may hold values from -6 to 6
- kernel: bfloat16 [64, 2, 2048, 768], P(None, None, 'seq', 'ch'), may hold values from -6 to 6
- fwd_inner: bfloat16 [64, 64], replicated, may hold values from -0.75 to 0.75
- fwd_middle: bfloat16 [64, 64], replicated, may hold values from -0.75 to 0.75
- fwd_outer: bfloat16 [64, 64], replicated, may hold values from -0.75 to 0.75
- inv_outer: bfloat16 [64, 64], replicated, may hold values from -0.75 to 0.75
- inv_middle: bfloat16 [64, 64], replicated, may hold values from -0.75 to 0.75
- inv_inner: bfloat16 [64, 64], replicated, may hold values from -0.75 to 0.75
- tw_inner: float32 [64, 64], replicated, may hold values from 0.5 to 1.5
- tw_middle: float32 [64, 64], replicated, may hold values from 0.5 to 1.5
- itw_middle: float32 [64, 64], replicated, may hold values from 0.5 to 1.5
- itw_inner: float32 [64, 64], replicated, may hold values from 0.5 to 1.5
- skip: float32 [768], P('ch'), may hold values from -1 to 1
- w_out: bfloat16 [768, 1536], P('ch'), may hold values from -0.21875 to 0.21875
Outputs:
- mixed: bfloat16 [262144, 1536], P('seq', 'ch')
All inputs are finite; a program needn't handle non-finite values.
Results may differ from a plain program's by a relative error of at most 0.0077.
Values may be sent and summed in bfloat16 or wider, within the bound.
A program may use at most 128 MiB of HBM per device.

v0:
```python
import jax
import jax.numpy as jnp
from jax import lax
from jax.sharding import PartitionSpec as P


def swapped(value, axis, distance):
    return lax.ppermute(value, axis, [(i, i ^ 1 << distance) for i in range(lax.axis_size(axis))])


def on_device(
    signal,
    gate,
    kernel,
    fwd_inner,
    fwd_middle,
    fwd_outer,
    inv_outer,
    inv_middle,
    inv_inner,
    tw_inner,
    tw_middle,
    itw_middle,
    itw_inner,
    skip,
    w_out,
):
    f32 = jnp.float32
    bf16 = jnp.bfloat16
    blk = fwd_inner.shape[0]
    half = blk // 2
    nchan = signal.shape[1]
    nseq = lax.axis_size("seq")
    outer = nseq // 2
    rows = blk * half // nseq
    position = lax.axis_index("seq")
    parity = position % 2
    outer_index = position // 2
    local = signal.reshape(half, blk, nchan)
    tw_rows = lax.dynamic_slice_in_dim(tw_inner, parity * half, half, 0)
    first = jnp.einsum("kc,bcn->bkn", fwd_inner, local, preferred_element_type=f32)
    first = (first * tw_rows[:, :, None]).astype(bf16).reshape(half, half, 2, nchan)
    keep = lax.dynamic_index_in_dim(first, parity, 2, False)
    sent = lax.dynamic_index_in_dim(first, 1 - parity, 2, False)
    partner = swapped(sent, "seq", 0)
    all_rows = jnp.where(
        parity == 0, jnp.concatenate([keep, partner], 0), jnp.concatenate([partner, keep], 0)
    )
    middle_row = lax.dynamic_slice_in_dim(tw_middle, outer_index, 1, 0)[0]
    second = jnp.einsum("jb,bmn->jmn", fwd_middle, all_rows, preferred_element_type=f32)
    second = (second * middle_row[:, None, None]).astype(bf16).reshape(1, blk * half, nchan)
    moved = lax.all_to_all(second, "seq", split_axis=1, concat_axis=0, tiled=True).reshape(
        outer, 2, rows, nchan
    )
    spectrum = jnp.einsum("ia,aprn->iprn", fwd_outer, moved, preferred_element_type=f32)
    spectrum = (spectrum * kernel.astype(f32)).astype(bf16)
    digit_b = (position * rows + jnp.arange(rows, dtype=jnp.int32)) // half
    select = (digit_b[:, None] == jnp.arange(blk, dtype=jnp.int32)[None, :]).astype(f32)
    factor = jnp.dot(itw_middle, select.T, precision=lax.Precision.HIGHEST)
    back_outer = jnp.einsum("ai,iprn->aprn", inv_outer, spectrum, preferred_element_type=f32)
    back_outer = (back_outer * factor[:, None, :, None]).astype(bf16).reshape(nseq, rows, nchan)
    returned = lax.all_to_all(back_outer, "seq", split_axis=0, concat_axis=1, tiled=True).reshape(
        blk, half, nchan
    )
    inner_cols = lax.dynamic_index_in_dim(itw_inner.reshape(blk, half, 2), parity, 2, False)
    back_middle = jnp.einsum("bj,jmn->bmn", inv_middle, returned, preferred_element_type=f32)
    back_middle = (back_middle * inner_cols[:, :, None]).astype(bf16)
    mine = lax.dynamic_slice_in_dim(back_middle, parity * half, half, 0)
    others = lax.dynamic_slice_in_dim(back_middle, (1 - parity) * half, half, 0)
    arrived = swapped(others, "seq", 0)
    joined = jnp.where(parity == 0, jnp.stack([mine, arrived], 2), jnp.stack([arrived, mine], 2))
    joined = joined.reshape(half, blk, nchan)
    conv = jnp.einsum("ck,bkn->bcn", inv_inner, joined, preferred_element_type=f32).reshape(
        half * blk, nchan
    )
    act = jax.nn.silu(gate.astype(f32)) * (conv + skip[None, :] * signal.astype(f32))
    act = act.astype(bf16)
    partial_out = jnp.dot(act, w_out, preferred_element_type=f32)
    total = lax.psum_scatter(partial_out, "ch", scatter_dimension=1, tiled=True)
    return total.astype(bf16)


def solution(mesh):
    placed = (
        P("seq", "ch"),
        P("seq", "ch"),
        P(None, None, "seq", "ch"),
        P(),
        P(),
        P(),
        P(),
        P(),
        P(),
        P(),
        P(),
        P(),
        P(),
        P("ch"),
        P("ch", None),
    )
    return jax.shard_map(
        on_device, mesh=mesh, in_specs=placed, out_specs=P("seq", "ch"), check_vma=False
    )
```

profile of v0, /device:TPU:1, one launch (start us, length us, event | category | flops | bytes accessed | tf_op | source)
XLA Modules:
  0.0 380.5 jit_solution(2593019773882750639)
XLA Ops:
  7.4 3.1 fusion.18
  10.5 3.5 reshape.61
  14.0 4.5 %constant_dynamic-slice_fusion.4 = (bf16[32,32,1,384]{3,2,1,0:T(2,128)(2,1)}, bf16[32,32,1,384]{3,2,1,0:T(2,128)(2,1)S(1)}) fusion(bf16[32,32,2,384]{3,2,1,0:T(2,128)(2,1)S(1)} %reshape.61, s32[]{:T(128)S(6)} %select_n.63, s32[]{:T(128)S(6)} %select_n.64), kind=kLoop, calls=%fused_computation.47 | loop fusion | bytes 3145736 | tf_op jit(solution)/shard_map/jit(dynamic_index_in_dim)/dynamic_slice | solution.py:43
  19.4 3.3 collective-permute-start
  22.7 1.7 copy.68
  25.1 2.6 fusion.19
  27.7 0.9 copy.41
  28.6 28.6 %copy.69 = bf16[1,2048,384]{2,0,1:T(2,128)(2,1)} copy(bf16[1,2048,384]{2,1,0:T(8,128)(2,1)S(1)} %bitcast.83) | data formatting | bytes 3145728 | tf_op jit(solution)/shard_map/reshape | solution.py:51
  57.7 34.2 %reduce = bf16[2048,384]{1,0:T(8,128)(2,1)S(1)} reduce(bf16[2048,1,384]{2,1,0:T(2,128)(2,1)} %bitcast.78, bf16[]{:T(256)} %broadcast.58), dimensions={1}, to_apply=%bitcast.77.reduce_sub_computation | reduce | bytes 3145730
  91.9 1.3 reshape.74
  93.2 12.1 %all-to-all-start = ((bf16[128,2,3072]{2,1,0:T(2,128)(2,1)}), bf16[128,2,3072]{2,1,0:T(2,128)(2,1)S(1)}, u32[]{:S(2)}, u32[]{:S(2)}) async-start(bf16[128,2,3072]{2,1,0:T(2,128)(2,1)} %reshape.74), calls=%async_computation | async-start | bytes 3145728 | tf_op jit(solution)/shard_map/all_to_all | solution.py:52
  105.6 39.5 %all-to-all-done = bf16[128,2,3072]{2,1,0:T(2,128)(2,1)S(1)} async-done(((bf16[128,2,3072]{2,1,0:T(2,128)(2,1)}), bf16[128,2,3072]{2,1,0:T(2,128)(2,1)S(1)}, u32[]{:S(2)}, u32[]{:S(2)}) %all-to-all-start) | async-done | bytes 1572896 | tf_op jit(solution)/shard_map/all_to_all | solution.py:52
  145.0 3.7 reshape.75
  148.8 3.3 copy.52
  152.1 4.0 %fusion.5 = bf16[64,2,16,384]{3,0,2,1:T(8,128)(2,1)S(1)} fusion(f32[64,16]{0,1:T(8,128)S(1)} %convolution_bitcast_fusion, bf16[64,2,16,384]{3,2,1,0:T(8,128)(2,1)} %param.17, bf16[64,2,16,384]{3,2,1,0:T(8,128)(2,1)} %bitcast.85, bf16[64,64]{1,0:T(8,128)(2,1)S(1)} %copy-done.10, bf16[64,64]{1,0:T(8,128)(2,1)S(1)} %copy-done.11), kind=kOutput, calls=%fused_computation.10 | convolution fusion | flops 205258752 | bytes 4739072 | tf_op jit(solution)/shard_map/ai,iprn->aprn/dot_general | solution.py:60
  156.1 2.1 copy.45
  158.2 8.2 %all-to-all-start.1 = ((bf16[128,16,384]{2,1,0:T(8,128)(2,1)}), bf16[128,16,384]{2,1,0:T(8,128)(2,1)S(1)}, u32[]{:S(2)}, u32[]{:S(2)}) async-start(bf16[128,16,384]{2,1,0:T(8,128)(2,1)} %bitcast.81), calls=%async_computation.1 | async-start | bytes 3145728 | tf_op jit(solution)/shard_map/all_to_all | solution.py:62
  166.5 39.5 %all-to-all-done.1 = bf16[128,16,384]{2,1,0:T(8,128)(2,1)S(1)} async-done(((bf16[128,16,384]{2,1,0:T(8,128)(2,1)}), bf16[128,16,384]{2,1,0:T(8,128)(2,1)S(1)}, u32[]{:S(2)}, u32[]{:S(2)}) %all-to-all-start.1) | async-done | bytes 1572896 | tf_op jit(solution)/shard_map/all_to_all | solution.py:62
  207.1 1.6 collective-permute-start.1
  208.7 1.9 collective-permute-done.1
  213.5 1.1 fusion.7
  214.7 6.3 %fusion.32 = f32[2048,1536]{1,0:T(8,128)} fusion(bf16[2048,384]{1,0:T(8,128)(2,1)S(1)} %fusion.7, bf16[384,1536]{1,0:T(8,128)(2,1)S(1)} %copy-done), kind=kOutput, calls=%fused_computation.55 | convolution fusion | flops 2415919104 | bytes 15335424 | tf_op jit(solution)/shard_map/dot_general | solution.py:78
  221.0 147.9 %reduce-scatter.2.cloned.1.call-done = f32[2048,768]{1,0:T(8,128)} async-done(((f32[2048,1536]{1,0:T(8,128)}), f32[2048,768]{1,0:T(8,128)}) %reduce-scatter.2.cloned.1.call-update) | async-done | bytes 6291472 | tf_op jit(solution)/shard_map/reduce_scatter | solution.py:79
  368.9 4.8 %convert_element_type.48 = bf16[2048,768]{1,0:T(8,128)(2,1)} convert(f32[2048,768]{1,0:T(8,128)} %reduce-scatter.2.cloned.1.call-done) | non-fusion elementwise | flops 1572864 | bytes 9437184 | tf_op jit(solution)/shard_map/convert_element_type | solution.py:80
  (40 shorter events, 7.1 us)
Async XLA Ops:
  6.5 208.1 %copy-start = (bf16[384,1536]{1,0:T(8,128)(2,1)S(1)}, bf16[384,1536]{1,0:T(8,128)(2,1)}, u32[]{:S(2)}) copy-start(bf16[384,1536]{1,0:T(8,128)(2,1)} %param.29) | copy-start | bytes 3538948
  18.5 4.2 %copy-start.2 = (bf16[32,32,1,384]{3,2,1,0:T(2,128)(2,1)S(1)}, bf16[32,32,1,384]{3,2,1,0:T(2,128)(2,1)}, u32[]{:S(2)}) copy-start(bf16[32,32,1,384]{3,2,1,0:T(2,128)(2,1)} %get-tuple-element.7) | copy-start | bytes 2359300
  19.3 5.8 %copy-start.9 = (bf16[64,64]{1,0:T(8,128)(2,1)S(1)}, bf16[64,64]{1,0:T(8,128)(2,1)}, u32[]{:S(2)}) copy-start(bf16[64,64]{1,0:T(8,128)(2,1)} %param.19) | copy-start | bytes 24580
  19.4 5.8 %collective-permute-start = (bf16[32,32,384]{2,0,1:T(8,128)(2,1)S(1)}, bf16[32,32,384]{2,0,1:T(8,128)(2,1)}, u32[]{:S(2)}, u32[]{:S(2)}) collective-permute-start(bf16[32,32,384]{2,0,1:T(8,128)(2,1)S(1)} %bitcast.86), channel_id=1, source_target_pairs={{0,2},{2,0},{4,6},{6,4},{8,10},{10,8},{12,14},{14,12},{16,18},{18,... | collective-permute-start | bytes 2359304 | tf_op jit(solution)/shard_map/ppermute | solution.py:8
  93.2 12.1 %copy-start.8 = (f32[64,64]{1,0:T(8,128)S(1)}, f32[64,64]{1,0:T(8,128)}, u32[]{:S(2)}) copy-start(f32[64,64]{1,0:T(8,128)} %param.26) | copy-start | bytes 49156
  93.2 51.8 %all-to-all-start = ((bf16[128,2,3072]{2,1,0:T(2,128)(2,1)}), bf16[128,2,3072]{2,1,0:T(2,128)(2,1)S(1)}, u32[]{:S(2)}, u32[]{:S(2)}) async-start(bf16[128,2,3072]{2,1,0:T(2,128)(2,1)} %reshape.74), calls=%async_computation | async-start | bytes 3145728 | tf_op jit(solution)/shard_map/all_to_all | solution.py:52
  148.8 3.3 copy-start.10
  148.8 3.3 copy-start.11
  158.1 8.3 %copy-start.4 = (f32[64,64]{1,0:T(8,128)S(1)}, f32[64,64]{1,0:T(8,128)}, u32[]{:S(2)}) copy-start(f32[64,64]{1,0:T(8,128)} %param.27) | copy-start | bytes 49156
  158.1 47.9 %copy-start.5 = (bf16[64,64]{1,0:T(8,128)(2,1)S(1)}, bf16[64,64]{1,0:T(8,128)(2,1)}, u32[]{:S(2)}) copy-start(bf16[64,64]{1,0:T(8,128)(2,1)} %param.22) | copy-start | bytes 24580
  158.2 47.9 %all-to-all-start.1 = ((bf16[128,16,384]{2,1,0:T(8,128)(2,1)}), bf16[128,16,384]{2,1,0:T(8,128)(2,1)S(1)}, u32[]{:S(2)}, u32[]{:S(2)}) async-start(bf16[128,16,384]{2,1,0:T(8,128)(2,1)} %bitcast.81), calls=%async_computation.1 | async-start | bytes 3145728 | tf_op jit(solution)/shard_map/all_to_all | solution.py:62
  166.4 202.6 %reduce-scatter.2.cloned.1.call-start = ((), (), s32[]{:S(2)}) async-start(), calls=%async_computation.3 | async-start | bytes 18874368 | tf_op jit(solution)/shard_map/reduce_scatter | solution.py:79
  207.1 3.6 collective-permute-start.1
  210.9 0.7 copy-start.6
  211.7 1.4 copy-start.1
  211.7 1.9 copy-start.3
  211.7 1.9 copy-start.7
Sparse Core Ops, SparseCore 0:
  221.2 147.7 reduce-scatter.1
where the time goes:
time: 381 us
  waiting for transfers between devices  229 us (60%)
  local copies, waits for them, and re-layouts  54.8 us (14%)
  other arithmetic  40.4 us (11%)
  starting transfers between devices  25.3 us (7%)
  matrix products  17.6 us (5%)
  between operations  13.6 us (4%)
    reduce_scatter x1, waiting for transfers between devices, on_device(): total = lax.psum_scatter(partial_out, 'ch', scatter_dimension=1, tiled=True)  148 us
    all_to_all x1, waiting for transfers between devices, on_device(): lax.all_to_all(back_outer, 'seq', split_axis=0, concat_axis=1, tiled=True)  39.5 us
    all_to_all x1, waiting for transfers between devices, on_device(): lax.all_to_all(second, 'seq', split_axis=1, concat_axis=0, tiled=True)  39.5 us
    unnamed x1, other arithmetic  34.2 us
    reshape x1, local copies, waits for them, and re-layouts, on_device(): (second * middle_row[:, None, None]).astype(bf16)  28.6 us
    all_to_all x1, starting transfers between devices, on_device(): lax.all_to_all(second, 'seq', split_axis=1, concat_axis=0, tiled=True)  12.1 us
    unnamed x29, local copies, waits for them, and re-layouts  10.6 us
    all_to_all x1, starting transfers between devices, on_device(): lax.all_to_all(back_outer, 'seq', split_axis=0, concat_axis=1, tiled=True)  8.22 us
  transfers between devices with their start and end apart: 5, of which 4 were waited for; matrix products, arithmetic and copies ran while one was open for 1% of the time, Pallas kernels for 0%

commit v1 on v0

v1 whole, which is shorter than its diff:
```python
import functools

import jax
import jax.numpy as jnp
from jax import lax
from jax.experimental import pallas as pl
from jax.experimental.pallas import tpu as pltpu
from jax.sharding import PartitionSpec as P

MESH = pl.DeviceIdType.MESH
F32 = jnp.float32
BF16 = jnp.bfloat16
LANES = 128
SUB = 16
NZ = 8
NXY = 8
NX = 4


def iota(shape, dim):
    return lax.broadcasted_iota(jnp.int32, shape, dim)


def one_hot(cond):
    return jnp.where(cond, 1.0, 0.0).astype(BF16)


def dot(a, b):
    return jnp.dot(a, b, preferred_element_type=F32)


def kernel(
    signal,
    gate,
    spectral,
    fwd_inner,
    fwd_middle,
    fwd_outer,
    inv_outer,
    inv_middle,
    inv_inner,
    tw_inner,
    tw_middle,
    itw_middle,
    itw_inner,
    skip,
    w_out,
    act_out,
    w_cat,
    sig,
    gat,
    ker,
    silu,
    rows_a,
    send_a,
    send_z,
    recv_z,
    recv_xy,
    spec,
    send_xy2,
    recv_xy2,
    recv_z2,
    send_j,
    rows_j,
    act,
    mat_in,
    mat_inv,
    mat_m,
    mat_f,
    mat_i,
    mat_im,
    t_in,
    t_mid,
    t_imid,
    t_iin,
    load_sem,
    local_sem,
    core_send,
    core_recv,
    z_send,
    z_recv,
    xy_send,
    xy_recv,
    xy2_send,
    xy2_recv,
    z2_send,
    z2_recv,
    core2_send,
    core2_recv,
    act_send,
    act_recv,
    w_send,
    w_recv,
    out_sem,
):
    nch = sig.shape[0]
    me = lax.axis_index("seq")
    ch = lax.axis_index("ch")
    core = me % 2
    chip = me // 2
    z = chip % NZ
    yx = chip // NZ
    y, x = yx // NX, yx % NX

    def at_z(d):
        other = (z + d) % NZ
        return other, ((yx * NZ + other) * 2 + core, ch)

    def at_xy(e):
        other = (y + e // NX) % 2 * NX + (x + e % NX) % NX
        return other, ((other * NZ + z) * 2 + core, ch)

    twin = (chip * 2 + 1 - core, ch)
    mate = (me, 1 - ch)

    def remote(src, dst, send, recv, device):
        return pltpu.make_async_remote_copy(
            src_ref=src,
            dst_ref=dst,
            send_sem=send,
            recv_sem=recv,
            device_id=device,
            device_id_type=MESH,
        )

    loads = []
    for i in range(nch):
        cols = pl.ds(i * LANES, LANES)
        trio = (
            pltpu.make_async_copy(signal.at[:, cols], sig.at[i], load_sem.at[0, i]),
            pltpu.make_async_copy(spectral.at[:, :, :, cols], ker.at[i], load_sem.at[1, i]),
            pltpu.make_async_copy(gate.at[:, cols], gat.at[i], load_sem.at[2, i]),
        )
        loads.append(trio)
    for kind in range(3):
        for i in range(nch):
            loads[i][kind].start()

    barrier = pltpu.get_barrier_semaphore()
    pl.semaphore_signal(barrier, inc=1, device_id=twin, device_id_type=MESH)
    pl.semaphore_signal(barrier, inc=1, device_id=mate, device_id_type=MESH)
    for d in range(1, NZ):
        pl.semaphore_signal(barrier, inc=1, device_id=at_z(d)[1], device_id_type=MESH)
    for e in range(1, NXY):
        pl.semaphore_signal(barrier, inc=1, device_id=at_xy(e)[1], device_id_type=MESH)

    def digit_k(q, flip):
        half = (q >> 5) ^ flip
        return 2 * (half * SUB + (q & 15)) + ((q >> 4) & 1)

    def expand(source, out, row_digit, col_digit, keep, block):
        size = out.shape[0]
        place = one_hot(iota((64, size), 0) == col_digit(iota((64, size), 1)))

        def body(n, carry):
            base = n * block
            pick = one_hot(iota((block, 64), 1) == row_digit(iota((block, 64), 0) + base))
            wide = dot(dot(pick, source[...]).astype(BF16), place)
            r = iota((block, size), 0) + base
            out[pl.ds(pl.multiple_of(base, block), block), :] = jnp.where(
                keep(r, iota((block, size), 1)), wide, 0.0
            ).astype(BF16)
            return carry

        lax.fori_loop(0, size // block, body, 0)

    def same_block(r, s):
        return (r >> 6) == (s >> 6)

    def same_sub(r, s):
        return (r & 15) == (s & 15)

    def in_z_order(q):
        return (q & 7) * 8 + (q >> 3)

    expand(fwd_inner, mat_in, lambda r: digit_k(r & 63, core), lambda s: s & 63, same_block, 128)

    def tw_in_body(n, carry):
        row = tw_inner[pl.ds(core * 32 + n, 1), :]
        hit = iota((64, 64), 1) == digit_k(iota((64, 64), 0), core)
        col = jnp.sum(jnp.where(hit, row, 0.0), axis=1, keepdims=True)
        t_in[pl.ds(pl.multiple_of(n * 64, 64), 64), :] = jnp.broadcast_to(col, (64, LANES))
        return carry

    lax.fori_loop(0, 32, tw_in_body, 0)

    def stage_inner(i):
        loads[i][0].wait()

        def body(n, carry):
            base = pl.multiple_of(n * 512, 512)
            wide = jnp.concatenate(
                [sig[i, pl.ds(base, 256), :], sig[i, pl.ds(base + 256, 256), :]], axis=1
            )
            res = dot(mat_in[...], wide)
            for s in range(2):
                part = res[:, s * LANES : (s + 1) * LANES] * t_in[pl.ds(base + 256 * s, 256), :]
                part = part.astype(BF16).reshape(4, 2, 2, SUB, LANES)
                b = n * 8 + s * 4
                rows_a[i, pl.ds(core * 32 + b, 4)] = part[:, 0]
                send_a[i, pl.ds(b, 4)] = part[:, 1]
            return carry

        lax.fori_loop(0, 4, body, 0)

    def core_copy(i):
        return remote(
            send_a.at[i],
            rows_a.at[i, pl.ds(core * 32, 32)],
            core_send.at[i],
            core_recv.at[i],
            twin,
        )

    stage_inner(0)
    pl.semaphore_wait(barrier, 2 + NZ - 1 + NXY - 1)
    core_copies = [core_copy(i) for i in range(nch)]
    core_copies[0].start()
    expand(fwd_middle, mat_m, lambda r: in_z_order(r >> 4), lambda s: s >> 4, same_sub, 128)
    tm_row = tw_middle[pl.ds(chip, 1), :]
    for n in range(4):
        hit = iota((256, 64), 1) == in_z_order((iota((256, 64), 0) + n * 256) >> 4)
        col = jnp.sum(jnp.where(hit, tm_row, 0.0), axis=1, keepdims=True)
        t_mid[n * 256 : (n + 1) * 256, :] = jnp.broadcast_to(col, (256, LANES))

    def pair(ref, i):
        v = ref[i].reshape(64, 2, SUB, LANES)
        return jnp.concatenate(
            [v[:, 0].reshape(64 * SUB, LANES), v[:, 1].reshape(64 * SUB, LANES)], axis=1
        )

    def apply(matrix, wide, finish):
        def body(n, carry):
            base = pl.multiple_of(n * 256, 256)
            finish(n, base, dot(matrix[pl.ds(base, 256), :], wide))
            return carry

        lax.fori_loop(0, 4, body, 0)

    def stage_middle(i):
        core_copies[i].wait_recv()

        def finish(n, base, res):
            for p in range(2):
                part = res[:, p * LANES : (p + 1) * LANES] * t_mid[pl.ds(base, 256), :]
                send_z[i, pl.ds(n * 2, 2), :, p] = part.astype(BF16).reshape(2, NXY, SUB, LANES)

        apply(mat_m, pair(rows_a, i), finish)

    order_z = (4, 3, 5, 2, 6, 1, 7)
    order_xy = (6, 2, 5, 7, 1, 3, 4)
    z_copies, xy_copies, xy2_copies, z2_copies = {}, {}, {}, {}

    def start_z(i):
        z_copies[i] = []
        for d in order_z:
            other, device = at_z(d)
            copy = remote(
                send_z.at[i, other], recv_z.at[i, z], z_send.at[i, d], z_recv.at[i, d], device
            )
            copy.start()
            z_copies[i].append(copy)
        own = pltpu.make_async_copy(send_z.at[i, z], recv_z.at[i, z], local_sem.at[0, i])
        own.start()
        z_copies[i].append(own)

    def start_xy(i):
        for copy in z_copies[i][:-1]:
            copy.wait_recv()
        z_copies[i][-1].wait()
        xy_copies[i] = []
        for e in order_xy:
            other, device = at_xy(e)
            copy = remote(
                recv_z.at[i, :, other],
                recv_xy.at[i, yx],
                xy_send.at[i, e],
                xy_recv.at[i, e],
                device,
            )
            copy.start()
            xy_copies[i].append(copy)
        own = pltpu.make_async_copy(recv_z.at[i, :, yx], recv_xy.at[i, yx], local_sem.at[1, i])
        own.start()
        xy_copies[i].append(own)

    def stage_outer(i):
        for copy in xy_copies[i][:-1]:
            copy.wait_recv()
        xy_copies[i][-1].wait()
        loads[i][1].wait()

        def product(n, base, res):
            factor = ker[i, pl.ds(n * 16, 16)]
            for p in range(2):
                part = res[:, p * LANES : (p + 1) * LANES].reshape(16, SUB, LANES)
                part = part * factor[:, p].astype(F32)
                spec[pl.ds(base, 256), p * LANES : (p + 1) * LANES] = part.astype(BF16).reshape(
                    256, LANES
                )

        apply(mat_f, pair(recv_xy, i), product)

        def finish(n, base, res):
            for p in range(2):
                part = res[:, p * LANES : (p + 1) * LANES] * t_imid[pl.ds(base, 256), :]
                send_xy2[i, pl.ds(n * 2, 2), :, p] = part.astype(BF16).reshape(2, NZ, SUB, LANES)

        apply(mat_i, spec[...], finish)

    def start_xy2(i):
        xy2_copies[i] = []
        for e in order_xy:
            other, device = at_xy(e)
            copy = remote(
                send_xy2.at[i, other],
                recv_xy2.at[i, yx],
                xy2_send.at[i, e],
                xy2_recv.at[i, e],
                device,
            )
            copy.start()
            xy2_copies[i].append(copy)
        own = pltpu.make_async_copy(send_xy2.at[i, yx], recv_xy2.at[i, yx], local_sem.at[2, i])
        own.start()
        xy2_copies[i].append(own)

    def start_z2(i):
        for copy in xy2_copies[i][:-1]:
            copy.wait_recv()
        xy2_copies[i][-1].wait()
        z2_copies[i] = []
        for d in order_z:
            other, device = at_z(d)
            copy = remote(
                recv_xy2.at[i, :, other],
                recv_z2.at[i, z],
                z2_send.at[i, d],
                z2_recv.at[i, d],
                device,
            )
            copy.start()
            z2_copies[i].append(copy)
        own = pltpu.make_async_copy(recv_xy2.at[i, :, z], recv_z2.at[i, z], local_sem.at[3, i])
        own.start()
        z2_copies[i].append(own)

    def core2_copy(i):
        return remote(
            send_j.at[i], rows_j.at[i, :, core], core2_send.at[i], core2_recv.at[i], twin
        )

    core2_copies = [core2_copy(i) for i in range(nch)]

    def stage_inv_middle(i):
        for copy in z2_copies[i][:-1]:
            copy.wait_recv()
        z2_copies[i][-1].wait()

        wide = pair(recv_z2, i)

        def block(n, target):
            base = pl.multiple_of(n * 256, 256)
            res = dot(mat_im[pl.ds(base, 256), :], wide)
            for p in range(2):
                part = res[:, p * LANES : (p + 1) * LANES] * t_iin[p, pl.ds(base, 256), :]
                target(n, p, part.astype(BF16).reshape(16, SUB, LANES))

        def to_twin(n, p, part):
            send_j[i, pl.ds((n - 2) * 16, 16), p] = part

        def to_own(n, p, part):
            rows_j[i, pl.ds(n * 16, 16), core, p] = part

        lax.fori_loop(2, 4, lambda n, c: (block(n, to_twin), c)[1], 0)
        core2_copies[i].start()
        lax.fori_loop(0, 2, lambda n, c: (block(n, to_own), c)[1], 0)

    act_copies = [
        remote(act.at[i], act_out.at[:, pl.ds((nch + i) * LANES, LANES)], act_send.at[i], act_recv.at[i], mate)
        for i in range(nch)
    ]
    own_outs = [
        pltpu.make_async_copy(act.at[i], act_out.at[:, pl.ds(i * LANES, LANES)], out_sem.at[i])
        for i in range(nch)
    ]

    def stage_inv_inner(i):
        core2_copies[i].wait_recv()
        scale = skip[0:1, i * LANES : (i + 1) * LANES]

        def body(n, carry):
            base = pl.multiple_of(n * 512, 512)
            left = rows_j[i, pl.ds(n * 8, 4)].reshape(256, LANES)
            right = rows_j[i, pl.ds(n * 8 + 4, 4)].reshape(256, LANES)
            res = dot(mat_inv[...], jnp.concatenate([left, right], axis=1))
            for s in range(2):
                at = pl.ds(base + 256 * s, 256)
                conv = res[:, s * LANES : (s + 1) * LANES]
                conv = conv + scale * sig[i, at, :].astype(F32)
                act[i, at, :] = (silu[i, at, :] * conv).astype(BF16)
            return carry

        lax.fori_loop(0, 4, body, 0)
        act_copies[i].start()
        own_outs[i].start()

    def make_silu(i):
        loads[i][2].wait()

        def body(n, carry):
            at = pl.ds(pl.multiple_of(n * 256, 256), 256)
            g = gat[i, at, :].astype(F32)
            silu[i, at, :] = g / (1.0 + jnp.exp(-g))
            return carry

        lax.fori_loop(0, 8, body, 0)

    def tw_imid_body(n, carry):
        row = itw_middle[pl.ds(n, 1), :]
        col = jnp.sum(jnp.where(iota((SUB, 64), 1) == chip, row, 0.0), axis=1, keepdims=True)
        t_imid[pl.ds(pl.multiple_of(n * SUB, SUB), SUB), :] = jnp.broadcast_to(col, (SUB, LANES))
        return carry

    def tw_iin_body(n, carry):
        row = itw_inner[pl.ds(((n >> 5) ^ core) * 32 + (n & 31), 1), :]
        for p in range(2):
            hit = iota((SUB, 64), 1) == 2 * (core * SUB + iota((SUB, 64), 0)) + p
            col = jnp.sum(jnp.where(hit, row, 0.0), axis=1, keepdims=True)
            t_iin[p, pl.ds(pl.multiple_of(n * SUB, SUB), SUB), :] = jnp.broadcast_to(
                col, (SUB, LANES)
            )
        return carry

    stage_middle(0)
    start_z(0)
    for i in range(1, nch):
        stage_inner(i)
        core_copies[i].start()
    width = w_cat.shape[1]
    w_copy = remote(
        w_out.at[:, pl.ds(pl.multiple_of((1 - ch) * width, width), width)],
        w_cat.at[pl.ds(w_out.shape[0], w_out.shape[0])],
        w_send,
        w_recv,
        mate,
    )
    w_copy.start()
    w_own = pltpu.make_async_copy(
        w_out.at[:, pl.ds(pl.multiple_of(ch * width, width), width)],
        w_cat.at[pl.ds(0, w_out.shape[0])],
        out_sem.at[nch],
    )
    w_own.start()
    stage_middle(1)
    start_z(1)
    stage_middle(2)
    expand(fwd_outer, mat_f, lambda r: r >> 4, lambda s: s >> 4, same_sub, 128)
    expand(inv_outer, mat_i, lambda r: r >> 4, lambda s: s >> 4, same_sub, 128)
    lax.fori_loop(0, 64, tw_imid_body, 0)
    start_xy(0)
    start_z(2)
    expand(
        inv_middle,
        mat_im,
        lambda r: (r >> 4) ^ (core * 32),
        lambda s: in_z_order(s >> 4),
        same_sub,
        128,
    )
    expand(inv_inner, mat_inv, lambda r: r & 63, lambda s: digit_k(s & 63, 0), same_block, 128)
    lax.fori_loop(0, 64, tw_iin_body, 0)
    stage_outer(0)
    start_xy2(0)
    for i in range(nch):
        make_silu(i)
    start_xy(1)
    start_z2(0)
    stage_outer(1)
    start_xy2(1)
    start_xy(2)
    start_z2(1)
    stage_outer(2)
    start_xy2(2)
    stage_inv_middle(0)
    stage_inv_inner(0)
    start_z2(2)
    stage_inv_middle(1)
    stage_inv_inner(1)
    stage_inv_middle(2)
    stage_inv_inner(2)

    for i in range(nch):
        core_copies[i].wait_send()
        core2_copies[i].wait_send()
        for table in (z_copies, xy_copies, xy2_copies, z2_copies):
            for copy in table[i][:-1]:
                copy.wait_send()
        own_outs[i].wait()
        act_copies[i].wait()
    w_own.wait()
    w_copy.wait()


def on_device(*args):
    signal, kernel_arr, skip, w_out = args[0], args[2], args[13], args[14]
    tokens, nchan = signal.shape
    nch = nchan // LANES
    width = w_out.shape[1] // 2
    small = pl.BlockSpec(memory_space=pltpu.VMEM)
    big = pl.BlockSpec(memory_space=pl.ANY)
    specs = [big, big, big] + [small] * 11 + [big]
    chunk = (nch, 64, 2, SUB, LANES)
    square = pltpu.VMEM((64 * SUB, 64 * SUB), BF16)
    dma = pltpu.SemaphoreType.DMA
    scratch = [
        pltpu.VMEM((nch, tokens, LANES), BF16),
        pltpu.VMEM((nch, tokens, LANES), BF16),
        pltpu.VMEM(chunk, BF16),
        pltpu.VMEM((nch, tokens, LANES), F32),
        pltpu.VMEM(chunk, BF16),
        pltpu.VMEM((nch, 32, 2, SUB, LANES), BF16),
        pltpu.VMEM((nch, NZ, NXY, 2, SUB, LANES), BF16),
        pltpu.VMEM((nch, NZ, NXY, 2, SUB, LANES), BF16),
        pltpu.VMEM((nch, NXY, NZ, 2, SUB, LANES), BF16),
        pltpu.VMEM((64 * SUB, 2 * LANES), BF16),
        pltpu.VMEM((nch, NXY, NZ, 2, SUB, LANES), BF16),
        pltpu.VMEM((nch, NXY, NZ, 2, SUB, LANES), BF16),
        pltpu.VMEM((nch, NZ, NXY, 2, SUB, LANES), BF16),
        pltpu.VMEM((nch, 32, 2, SUB, LANES), BF16),
        pltpu.VMEM((nch, 32, 2, 2, SUB, LANES), BF16),
        pltpu.VMEM((nch, tokens, LANES), BF16),
        pltpu.VMEM((256, 256), BF16),
        pltpu.VMEM((256, 256), BF16),
        square,
        square,
        square,
        square,
        pltpu.VMEM((tokens, LANES), F32),
        pltpu.VMEM((64 * SUB, LANES), F32),
        pltpu.VMEM((64 * SUB, LANES), F32),
        pltpu.VMEM((2, 64 * SUB, LANES), F32),
        dma((3, nch)),
        dma((4, nch)),
        dma((nch,)),
        dma((nch,)),
        dma((nch, NZ)),
        dma((nch, NZ)),
        dma((nch, NXY)),
        dma((nch, NXY)),
        dma((nch, NXY)),
        dma((nch, NXY)),
        dma((nch, NZ)),
        dma((nch, NZ)),
        dma((nch,)),
        dma((nch,)),
        dma((nch,)),
        dma((nch,)),
        dma(()),
        dma(()),
        dma((nch + 1,)),
    ]
    operands = list(args)
    operands[13] = skip.reshape(1, nchan)
    act, w_cat = pl.pallas_call(
        kernel,
        out_shape=(
            jax.ShapeDtypeStruct((tokens, 2 * nchan), BF16),
            jax.ShapeDtypeStruct((2 * nchan, width), BF16),
        ),
        in_specs=specs,
        out_specs=(big, big),
        scratch_shapes=scratch,
        compiler_params=pltpu.CompilerParams(
            collective_id=0, has_side_effects=True, vmem_limit_bytes=56 * 2**20
        ),
    )(*operands)
    return jnp.dot(act, w_cat, preferred_element_type=F32).astype(BF16)


def solution(mesh):
    placed = (
        P("seq", "ch"),
        P("seq", "ch"),
        P(None, None, "seq", "ch"),
        P(),
        P(),
        P(),
        P(),
        P(),
        P(),
        P(),
        P(),
        P(),
        P(),
        P("ch"),
        P("ch", None),
    )
    return jax.shard_map(
        on_device, mesh=mesh, in_specs=placed, out_specs=P("seq", "ch"), check_vma=False
    )
```

time: 381 us -> 124 us (0.33)
  waiting for transfers between devices: 229 us -> 0 us
  Pallas kernels: 0 us -> 116 us
  local copies, waits for them, and re-layouts: 54.8 us -> 1.24 us
  other arithmetic: 40.4 us -> 0 us
  starting transfers between devices: 25.3 us -> 0 us
  between operations: 13.6 us -> 0.01 us
  matrix products: 17.6 us -> 6.51 us
    reduce_scatter x1 -> x0, waiting for transfers between devices: 148 us -> none  [on_device(): total = lax.psum_scatter(partial_out, 'ch', scatter_dimension=1, tiled=True)]
    pallas_call x0 -> x1, Pallas kernels: none -> 116 us  [on_device(): pl.pallas_call(kernel, out_shape=(jax.ShapeDtypeStruct((tokens, 2 * nchan...]
    all_to_all x2 -> x0, waiting for transfers between devices: 79 us -> none  [the longest x1 39.5 us: on_device(): lax.all_to_all(back_outer, 'seq', split_axis=0, concat_axis=1, tiled=True)]
    unnamed x1 -> x0, other arithmetic: 34.2 us -> none
    reshape x2 -> x1, local copies, waits for them, and re-layouts: 32.1 us -> 1.24 us  [on_device(): operands[13] = skip.reshape(1, nchan)]
    all_to_all x2 -> x0, starting transfers between devices: 20.3 us -> none  [the longest x1 12.1 us: on_device(): lax.all_to_all(second, 'seq', split_axis=1, concat_axis=0, tiled=True)]
    dot_general x7 -> x1, matrix products: 17.6 us -> 6.51 us  [on_device(): return jnp.dot(act, w_cat, preferred_element_type=F32).astype(BF16)]
    unnamed x29 -> x0, local copies, waits for them, and re-layouts: 10.6 us -> none
  transfers between devices with their start and end apart: 5 -> 0, of which waited for: 4 -> 0; matrix products, arithmetic and copies ran while one was open for 1% -> 0% of each run, Pallas kernels for 0% -> 0%
where the time goes in v1:
time: 124 us
  Pallas kernels  116 us (94%)
  matrix products  6.51 us (5%)
  local copies, waits for them, and re-layouts  1.24 us (1%)
    pallas_call x1, Pallas kernels, on_device(): pl.pallas_call(kernel, out_shape=(jax.ShapeDtypeStruct((tokens, 2 * nchan...  116 us
    dot_general x1, matrix products, on_device(): return jnp.dot(act, w_cat, preferred_element_type=F32).astype(BF16)  6.51 us

profile of v1, /device:TPU:1, one launch (start us, length us, event | category | flops | bytes accessed | tf_op | source)
XLA Modules:
  0.0 123.7 jit_solution(8210862403209694914)
XLA Ops:
  0.0 1.2 %reshape.3.skip = f32[1,384]{1,0:T(1,128)} reshape(f32[384]{0:T(512)} %param.28) | data formatting | bytes 3072 | tf_op jit(solution)/shard_map/reshape | solution.py:564
  1.2 116.0 %shard_map.145 = (bf16[2048,768]{1,0:T(8,128)(2,1)}, bf16[768,768]{1,0:T(8,128)(2,1)}) custom-call(bf16[2048,384]{1,0:T(8,128)(2,1)} %signal.1, bf16[2048,384]{1,0:T(8,128)(2,1)} %gate.1, bf16[64,2,16,384]{3,2,1,0:T(8,128)(2,1)} %spectral.1, bf16[64,64]{1,0:T(8,128)(2,1)} %fwd_inner.1, bf16[64,64]{1,0:T(8,128)(2,1)} %fwd_middle.1, bf16[64,64]{1,0:T(8,128)(2,1)} %fwd_outer.1, ...), custom_call_target="tpu_custom_call" | custom-call | tf_op jit(solution)/shard_map/pallas_call | solution.py:565
  117.2 6.5 %convolution_convert_fusion = bf16[2048,768]{1,0:T(8,128)(2,1)} fusion(bf16[2048,768]{1,0:T(8,128)(2,1)} %get-tuple-element.7, bf16[768,768]{1,0:T(8,128)(2,1)} %get-tuple-element.8), kind=kOutput, calls=%fused_computation | convolution fusion | flops 2417491968 | bytes 7471104 | tf_op jit(solution)/shard_map/dot_general | solution.py:578

commit v2 on v1

--- a/solution.py
+++ b/solution.py
@@ -1,5 +1,3 @@
-import functools
-
 import jax
 import jax.numpy as jnp
 from jax import lax
@@ -15,6 +13,8 @@
 NZ = 8
 NXY = 8
 NX = 4
+ROWS = 512
+BAND = 512
 
 
 def iota(shape, dim):
@@ -33,20 +33,19 @@
     signal,
     gate,
     spectral,
-    fwd_inner,
-    fwd_middle,
-    fwd_outer,
-    inv_outer,
-    inv_middle,
-    inv_inner,
-    tw_inner,
-    tw_middle,
-    itw_middle,
-    itw_inner,
+    fwd_inner_hbm,
+    fwd_middle_hbm,
+    fwd_outer_hbm,
+    inv_outer_hbm,
+    inv_middle_hbm,
+    inv_inner_hbm,
+    tw_inner_hbm,
+    tw_middle_hbm,
+    itw_middle_hbm,
+    itw_inner_hbm,
     skip,
     w_out,
-    act_out,
-    w_cat,
+    out,
     sig,
     gat,
     ker,
@@ -73,6 +72,15 @@
     t_mid,
     t_imid,
     t_iin,
+    factors,
+    twiddles,
+    wide_factor,
+    column,
+    act_in,
+    weights,
+    total,
+    staged,
+    small_sem,
     load_sem,
     local_sem,
     core_send,
@@ -123,6 +131,26 @@
             device_id_type=MESH,
         )
 
+    fwd_inner, fwd_middle, fwd_outer, inv_outer, inv_middle, inv_inner = range(6)
+    tw_inner, tw_middle, itw_middle, itw_inner = (twiddles.at[n] for n in range(4))
+    given = (
+        fwd_inner_hbm,
+        fwd_middle_hbm,
+        fwd_outer_hbm,
+        inv_outer_hbm,
+        inv_middle_hbm,
+        inv_inner_hbm,
+    )
+    given_tw = (tw_inner_hbm, tw_middle_hbm, itw_middle_hbm, itw_inner_hbm)
+    factor_loads = [
+        pltpu.make_async_copy(ref, factors.at[n], small_sem.at[n]) for n, ref in enumerate(given)
+    ]
+    tw_loads = [
+        pltpu.make_async_copy(ref, twiddles.at[n], small_sem.at[6 + n])
+        for n, ref in enumerate(given_tw)
+    ]
+    factor_loads[0].start()
+    tw_loads[0].start()
     loads = []
     for i in range(nch):
         cols = pl.ds(i * LANES, LANES)
@@ -132,9 +160,11 @@
             pltpu.make_async_copy(gate.at[:, cols], gat.at[i], load_sem.at[2, i]),
         )
         loads.append(trio)
-    for kind in range(3):
-        for i in range(nch):
-            loads[i][kind].start()
+    loads[0][0].start()
+    for copy in factor_loads[1:] + tw_loads[1:]:
+        copy.start()
+    for i in range(1, nch):
+        loads[i][0].start()
 
     barrier = pltpu.get_barrier_semaphore()
     pl.semaphore_signal(barrier, inc=1, device_id=twin, device_id_type=MESH)
@@ -148,41 +178,50 @@
         half = (q >> 5) ^ flip
         return 2 * (half * SUB + (q & 15)) + ((q >> 4) & 1)
 
-    def expand(source, out, row_digit, col_digit, keep, block):
-        size = out.shape[0]
-        place = one_hot(iota((64, size), 0) == col_digit(iota((64, size), 1)))
-
-        def body(n, carry):
-            base = n * block
-            pick = one_hot(iota((block, 64), 1) == row_digit(iota((block, 64), 0) + base))
-            wide = dot(dot(pick, source[...]).astype(BF16), place)
-            r = iota((block, size), 0) + base
-            out[pl.ds(pl.multiple_of(base, block), block), :] = jnp.where(
-                keep(r, iota((block, size), 1)), wide, 0.0
-            ).astype(BF16)
-            return carry
-
-        lax.fori_loop(0, size // block, body, 0)
-
-    def same_block(r, s):
-        return (r >> 6) == (s >> 6)
-
-    def same_sub(r, s):
-        return (r & 15) == (s & 15)
-
     def in_z_order(q):
         return (q & 7) * 8 + (q >> 3)
 
-    expand(fwd_inner, mat_in, lambda r: digit_k(r & 63, core), lambda s: s & 63, same_block, 128)
-
-    def tw_in_body(n, carry):
-        row = tw_inner[pl.ds(core * 32 + n, 1), :]
-        hit = iota((64, 64), 1) == digit_k(iota((64, 64), 0), core)
-        col = jnp.sum(jnp.where(hit, row, 0.0), axis=1, keepdims=True)
-        t_in[pl.ds(pl.multiple_of(n * 64, 64), 64), :] = jnp.broadcast_to(col, (64, LANES))
+    diagonal = iota((SUB, 64 * SUB), 0) == (iota((SUB, 64 * SUB), 1) & 15)
+
+    def expand(n, out, row_digit, col_digit):
+        factor_loads[n].wait()
+        place = one_hot(iota((64, 64 * SUB), 0) == col_digit(iota((64, 64 * SUB), 1) >> 4))
+        wide_factor[...] = dot(factors[n], place)
+
+        def body(t, carry):
+            for u in range(8):
+                q = t * 8 + u
+                row = jnp.broadcast_to(wide_factor[pl.ds(row_digit(q), 1), :], (SUB, 64 * SUB))
+                out[pl.ds(pl.multiple_of(q * SUB, SUB), SUB), :] = jnp.where(
+                    diagonal, row, 0.0
+                ).astype(BF16)
+            return carry
+
+        lax.fori_loop(0, 8, body, 0)
+
+    def expand_four(n, out, row_digit, col_digit):
+        factor_loads[n].wait()
+        place = one_hot(iota((64, 256), 0) == col_digit(iota((64, 256), 1) & 63))
+        pick = one_hot(iota((64, 64), 1) == row_digit(iota((64, 64), 0)))
+        wide = dot(dot(pick, factors[n]).astype(BF16), place)
+        for b in range(4):
+            out[b * 64 : (b + 1) * 64, :] = jnp.where(
+                (iota((64, 256), 1) >> 6) == b, wide, 0.0
+            ).astype(BF16)
+
+    expand_four(fwd_inner, mat_in, lambda r: digit_k(r, core), lambda s: s)
+    tw_loads[0].wait()
+    in_hit = iota((64, 64), 1) == digit_k(iota((64, 64), 0), core)
+
+    def tw_in_body(t, carry):
+        for u in range(8):
+            n = t * 8 + u
+            row = tw_inner[pl.ds(core * 32 + n, 1), :]
+            col = jnp.sum(jnp.where(in_hit, row, 0.0), axis=1, keepdims=True)
+            t_in[pl.ds(pl.multiple_of(n * 64, 64), 64), :] = jnp.broadcast_to(col, (64, LANES))
         return carry
 
-    lax.fori_loop(0, 32, tw_in_body, 0)
+    lax.fori_loop(0, 4, tw_in_body, 0)
 
     def stage_inner(i):
         loads[i][0].wait()
@@ -216,7 +255,12 @@
     pl.semaphore_wait(barrier, 2 + NZ - 1 + NXY - 1)
     core_copies = [core_copy(i) for i in range(nch)]
     core_copies[0].start()
-    expand(fwd_middle, mat_m, lambda r: in_z_order(r >> 4), lambda s: s >> 4, same_sub, 128)
+    for i in range(nch):
+        loads[i][1].start()
+    stage_inner(1)
+    core_copies[1].start()
+    expand(fwd_middle, mat_m, in_z_order, lambda s: s)
+    tw_loads[1].wait()
     tm_row = tw_middle[pl.ds(chip, 1), :]
     for n in range(4):
         hit = iota((256, 64), 1) == in_z_order((iota((256, 64), 0) + n * 256) >> 4)
@@ -231,19 +275,19 @@
 
     def apply(matrix, wide, finish):
         def body(n, carry):
-            base = pl.multiple_of(n * 256, 256)
-            finish(n, base, dot(matrix[pl.ds(base, 256), :], wide))
-            return carry
-
-        lax.fori_loop(0, 4, body, 0)
+            base = pl.multiple_of(n * BAND, BAND)
+            finish(n, base, dot(matrix[pl.ds(base, BAND), :], wide))
+            return carry
+
+        lax.fori_loop(0, 64 * SUB // BAND, body, 0)
 
     def stage_middle(i):
         core_copies[i].wait_recv()
 
         def finish(n, base, res):
             for p in range(2):
-                part = res[:, p * LANES : (p + 1) * LANES] * t_mid[pl.ds(base, 256), :]
-                send_z[i, pl.ds(n * 2, 2), :, p] = part.astype(BF16).reshape(2, NXY, SUB, LANES)
+                part = res[:, p * LANES : (p + 1) * LANES] * t_mid[pl.ds(base, BAND), :]
+                send_z[i, pl.ds(n * 4, 4), :, p] = part.astype(BF16).reshape(4, NXY, SUB, LANES)
 
         apply(mat_m, pair(rows_a, i), finish)
 
@@ -291,20 +335,20 @@
         loads[i][1].wait()
 
         def product(n, base, res):
-            factor = ker[i, pl.ds(n * 16, 16)]
+            factor = ker[i, pl.ds(n * 32, 32)]
             for p in range(2):
-                part = res[:, p * LANES : (p + 1) * LANES].reshape(16, SUB, LANES)
+                part = res[:, p * LANES : (p + 1) * LANES].reshape(32, SUB, LANES)
                 part = part * factor[:, p].astype(F32)
-                spec[pl.ds(base, 256), p * LANES : (p + 1) * LANES] = part.astype(BF16).reshape(
-                    256, LANES
+                spec[pl.ds(base, BAND), p * LANES : (p + 1) * LANES] = part.astype(BF16).reshape(
+                    BAND, LANES
                 )
 
         apply(mat_f, pair(recv_xy, i), product)
 
         def finish(n, base, res):
             for p in range(2):
-                part = res[:, p * LANES : (p + 1) * LANES] * t_imid[pl.ds(base, 256), :]
-                send_xy2[i, pl.ds(n * 2, 2), :, p] = part.astype(BF16).reshape(2, NZ, SUB, LANES)
+                part = res[:, p * LANES : (p + 1) * LANES] * t_imid[pl.ds(base, BAND), :]
+                send_xy2[i, pl.ds(n * 4, 4), :, p] = part.astype(BF16).reshape(4, NZ, SUB, LANES)
 
         apply(mat_i, spec[...], finish)
 
@@ -376,18 +420,15 @@
         core2_copies[i].start()
         lax.fori_loop(0, 2, lambda n, c: (block(n, to_own), c)[1], 0)
 
-    act_copies = [
-        remote(act.at[i], act_out.at[:, pl.ds((nch + i) * LANES, LANES)], act_send.at[i], act_recv.at[i], mate)
-        for i in range(nch)
-    ]
-    own_outs = [
-        pltpu.make_async_copy(act.at[i], act_out.at[:, pl.ds(i * LANES, LANES)], out_sem.at[i])
-        for i in range(nch)
-    ]
+    def act_copy(i, n):
+        at = pl.ds(pl.multiple_of(n * ROWS, ROWS), ROWS)
+        return remote(
+            act.at[i, at], act_in.at[i, at], act_send.at[i, n], act_recv.at[i, n], mate
+        )
 
     def stage_inv_inner(i):
         core2_copies[i].wait_recv()
-        scale = skip[0:1, i * LANES : (i + 1) * LANES]
+        scale = skip[pl.ds(i * LANES, LANES)].reshape(1, LANES)
 
         def body(n, carry):
             base = pl.multiple_of(n * 512, 512)
@@ -399,11 +440,35 @@
                 conv = res[:, s * LANES : (s + 1) * LANES]
                 conv = conv + scale * sig[i, at, :].astype(F32)
                 act[i, at, :] = (silu[i, at, :] * conv).astype(BF16)
+            act_copy(i, n).start()
             return carry
 
         lax.fori_loop(0, 4, body, 0)
-        act_copies[i].start()
-        own_outs[i].start()
+
+    def out_copy(n):
+        at = pl.ds(pl.multiple_of(n * ROWS, ROWS), ROWS)
+        return pltpu.make_async_copy(staged.at[at], out.at[at], out_sem.at[n])
+
+    def project(step, parts):
+        def body(n, carry):
+            at = pl.ds(pl.multiple_of(n * ROWS, ROWS), ROWS)
+            for ref, i in parts:
+                if ref is act_in:
+                    act_copy(i, n).wait_recv()
+            wide = jnp.concatenate([ref[i, at, :] for ref, i in parts], axis=1)
+            for c in range(0, width, 256):
+                res = dot(wide, weights[step * 256 : (step + 1) * 256, c : c + 256])
+                if step > 0:
+                    res = res + total[at, c : c + 256]
+                if step < 2:
+                    total[at, c : c + 256] = res
+                else:
+                    staged[at, c : c + 256] = res.astype(BF16)
+            if step == 2:
+                out_copy(n).start()
+            return carry
+
+        lax.fori_loop(0, sig.shape[1] // ROWS, body, 0)
 
     def make_silu(i):
         loads[i][2].wait()
@@ -416,31 +481,49 @@
 
         lax.fori_loop(0, 8, body, 0)
 
-    def tw_imid_body(n, carry):
-        row = itw_middle[pl.ds(n, 1), :]
-        col = jnp.sum(jnp.where(iota((SUB, 64), 1) == chip, row, 0.0), axis=1, keepdims=True)
-        t_imid[pl.ds(pl.multiple_of(n * SUB, SUB), SUB), :] = jnp.broadcast_to(col, (SUB, LANES))
-        return carry
-
-    def tw_iin_body(n, carry):
-        row = itw_inner[pl.ds(((n >> 5) ^ core) * 32 + (n & 31), 1), :]
-        for p in range(2):
-            hit = iota((SUB, 64), 1) == 2 * (core * SUB + iota((SUB, 64), 0)) + p
-            col = jnp.sum(jnp.where(hit, row, 0.0), axis=1, keepdims=True)
-            t_iin[p, pl.ds(pl.multiple_of(n * SUB, SUB), SUB), :] = jnp.broadcast_to(
-                col, (SUB, LANES)
-            )
-        return carry
+    def tw_imid():
+        tw_loads[2].wait()
+        hit = iota((64, 64), 1) == chip
+        col = jnp.sum(jnp.where(hit, itw_middle[...], 0.0), axis=1, keepdims=True)
+        column[...] = jnp.broadcast_to(col, (64, LANES))
+
+        def body(t, carry):
+            for u in range(8):
+                n = t * 8 + u
+                t_imid[pl.ds(pl.multiple_of(n * SUB, SUB), SUB), :] = jnp.broadcast_to(
+                    column[pl.ds(n, 1), :], (SUB, LANES)
+                )
+            return carry
+
+        lax.fori_loop(0, 8, body, 0)
+
+    def tw_iin():
+        tw_loads[3].wait()
+        hits = [
+            iota((SUB, 64), 1) == 2 * (core * SUB + iota((SUB, 64), 0)) + p for p in range(2)
+        ]
+
+        def body(t, carry):
+            for u in range(8):
+                n = t * 8 + u
+                row = itw_inner[pl.ds((t // 4 + core) % 2 * 32 + n % 32, 1), :]
+                for p in range(2):
+                    col = jnp.sum(jnp.where(hits[p], row, 0.0), axis=1, keepdims=True)
+                    t_iin[p, pl.ds(pl.multiple_of(n * SUB, SUB), SUB), :] = jnp.broadcast_to(
+                        col, (SUB, LANES)
+                    )
+            return carry
+
+        lax.fori_loop(0, 8, body, 0)
 
     stage_middle(0)
     start_z(0)
-    for i in range(1, nch):
-        stage_inner(i)
-        core_copies[i].start()
-    width = w_cat.shape[1]
+    stage_inner(2)
+    core_copies[2].start()
+    depth, width = weights.shape[0] // 2, weights.shape[1]
     w_copy = remote(
         w_out.at[:, pl.ds(pl.multiple_of((1 - ch) * width, width), width)],
-        w_cat.at[pl.ds(w_out.shape[0], w_out.shape[0])],
+        weights.at[pl.ds(depth, depth)],
         w_send,
         w_recv,
         mate,
@@ -448,36 +531,31 @@
     w_copy.start()
     w_own = pltpu.make_async_copy(
         w_out.at[:, pl.ds(pl.multiple_of(ch * width, width), width)],
-        w_cat.at[pl.ds(0, w_out.shape[0])],
-        out_sem.at[nch],
+        weights.at[pl.ds(0, depth)],
+        small_sem.at[10],
     )
     w_own.start()
+    for i in range(nch):
+        loads[i][2].start()
     stage_middle(1)
+    stage_middle(2)
+    expand(fwd_outer, mat_f, lambda q: q, lambda s: s)
+    expand(inv_outer, mat_i, lambda q: q, lambda s: s)
+    tw_imid()
     start_z(1)
-    stage_middle(2)
-    expand(fwd_outer, mat_f, lambda r: r >> 4, lambda s: s >> 4, same_sub, 128)
-    expand(inv_outer, mat_i, lambda r: r >> 4, lambda s: s >> 4, same_sub, 128)
-    lax.fori_loop(0, 64, tw_imid_body, 0)
     start_xy(0)
-    start_z(2)
-    expand(
-        inv_middle,
-        mat_im,
-        lambda r: (r >> 4) ^ (core * 32),
-        lambda s: in_z_order(s >> 4),
-        same_sub,
-        128,
-    )
-    expand(inv_inner, mat_inv, lambda r: r & 63, lambda s: digit_k(s & 63, 0), same_block, 128)
-    lax.fori_loop(0, 64, tw_iin_body, 0)
+    expand(inv_middle, mat_im, lambda q: (q // 32 + core) % 2 * 32 + q % 32, in_z_order)
+    expand_four(inv_inner, mat_inv, lambda r: r, lambda s: digit_k(s, 0))
+    tw_iin()
+    for i in range(nch):
+        make_silu(i)
     stage_outer(0)
     start_xy2(0)
-    for i in range(nch):
-        make_silu(i)
+    start_z(2)
     start_xy(1)
-    start_z2(0)
     stage_outer(1)
     start_xy2(1)
+    start_z2(0)
     start_xy(2)
     start_z2(1)
     stage_outer(2)
@@ -485,10 +563,15 @@
     stage_inv_middle(0)
     stage_inv_inner(0)
     start_z2(2)
+    w_own.wait()
     stage_inv_middle(1)
     stage_inv_inner(1)
+    project(0, ((act, 0), (act, 1)))
     stage_inv_middle(2)
     stage_inv_inner(2)
+    w_copy.wait_recv()
+    project(1, ((act, 2), (act_in, 0)))
+    project(2, ((act_in, 1), (act_in, 2)))
 
     for i in range(nch):
         core_copies[i].wait_send()
@@ -496,20 +579,20 @@
         for table in (z_copies, xy_copies, xy2_copies, z2_copies):
             for copy in table[i][:-1]:
                 copy.wait_send()
-        own_outs[i].wait()
-        act_copies[i].wait()
-    w_own.wait()
-    w_copy.wait()
+        for n in range(sig.shape[1] // ROWS):
+            act_copy(i, n).wait_send()
+    w_copy.wait_send()
+    for n in range(sig.shape[1] // ROWS):
+        out_copy(n).wait()
 
 
 def on_device(*args):
-    signal, kernel_arr, skip, w_out = args[0], args[2], args[13], args[14]
+    signal, w_out = args[0], args[14]
     tokens, nchan = signal.shape
     nch = nchan // LANES
     width = w_out.shape[1] // 2
-    small = pl.BlockSpec(memory_space=pltpu.VMEM)
     big = pl.BlockSpec(memory_space=pl.ANY)
-    specs = [big, big, big] + [small] * 11 + [big]
+    specs = [big] * 13 + [pl.BlockSpec(memory_space=pltpu.VMEM), big]
     chunk = (nch, 64, 2, SUB, LANES)
     square = pltpu.VMEM((64 * SUB, 64 * SUB), BF16)
     dma = pltpu.SemaphoreType.DMA
@@ -540,6 +623,15 @@
         pltpu.VMEM((64 * SUB, LANES), F32),
         pltpu.VMEM((64 * SUB, LANES), F32),
         pltpu.VMEM((2, 64 * SUB, LANES), F32),
+        pltpu.VMEM((6, 64, 64), BF16),
+        pltpu.VMEM((4, 64, 64), F32),
+        pltpu.VMEM((64, 64 * SUB), F32),
+        pltpu.VMEM((64, LANES), F32),
+        pltpu.VMEM((nch, tokens, LANES), BF16),
+        pltpu.VMEM((2 * nchan, width), BF16),
+        pltpu.VMEM((tokens, width), F32),
+        pltpu.VMEM((tokens, width), BF16),
+        dma((11,)),
         dma((3, nch)),
         dma((4, nch)),
         dma((nch,)),
@@ -554,28 +646,22 @@
         dma((nch, NZ)),
         dma((nch,)),
         dma((nch,)),
-        dma((nch,)),
-        dma((nch,)),
+        dma((nch, tokens // ROWS)),
+        dma((nch, tokens // ROWS)),
         dma(()),
         dma(()),
-        dma((nch + 1,)),
+        dma((tokens // ROWS,)),
     ]
-    operands = list(args)
-    operands[13] = skip.reshape(1, nchan)
-    act, w_cat = pl.pallas_call(
+    return pl.pallas_call(
         kernel,
-        out_shape=(
-            jax.ShapeDtypeStruct((tokens, 2 * nchan), BF16),
-            jax.ShapeDtypeStruct((2 * nchan, width), BF16),
-        ),
+        out_shape=jax.ShapeDtypeStruct((tokens, width), BF16),
         in_specs=specs,
-        out_specs=(big, big),
+        out_specs=big,
         scratch_shapes=scratch,
         compiler_params=pltpu.CompilerParams(
             collective_id=0, has_side_effects=True, vmem_limit_bytes=56 * 2**20
         ),
-    )(*operands)
-    return jnp.dot(act, w_cat, preferred_element_type=F32).astype(BF16)
+    )(*args)
 
 
 def solution(mesh):

time: 124 us -> 112 us (0.903)
  Pallas kernels: 116 us -> 108 us
  matrix products: 6.51 us -> 0 us
  local copies, waits for them, and re-layouts: 1.24 us -> 3.76 us
    pallas_call x1, Pallas kernels: 116 us -> 108 us  [on_device(): pl.pallas_call(kernel, out_shape=jax.ShapeDtypeStruct((tokens, width), BF...]
    dot_general x1 -> x0, matrix products: 6.51 us -> none  [on_device(): return jnp.dot(act, w_cat, preferred_element_type=F32).astype(BF16)]
    unnamed x0 -> x1, local copies, waits for them, and re-layouts: none -> 3.76 us
    reshape x1 -> x0, local copies, waits for them, and re-layouts: 1.24 us -> none  [on_device(): operands[13] = skip.reshape(1, nchan)]
where the time goes in v2:
time: 112 us
  Pallas kernels  108 us (96%)
  local copies, waits for them, and re-layouts  3.76 us (3%)
    pallas_call x1, Pallas kernels, on_device(): pl.pallas_call(kernel, out_shape=jax.ShapeDtypeStruct((tokens, width), BF...  108 us
    unnamed x1, local copies, waits for them, and re-layouts  3.76 us

profile of v2, /device:TPU:1, one launch (start us, length us, event | category | flops | bytes accessed | tf_op | source)
XLA Modules:
  0.0 111.9 jit_solution(934313875651267368)
XLA Ops:
  0.0 108.1 %shard_map.145 = bf16[2048,768]{1,0:T(8,128)(2,1)} custom-call(bf16[2048,384]{1,0:T(8,128)(2,1)} %signal.1, bf16[2048,384]{1,0:T(8,128)(2,1)} %gate.1, bf16[64,2,16,384]{3,2,1,0:T(8,128)(2,1)} %spectral.1, bf16[64,64]{1,0:T(8,128)(2,1)} %fwd_inner_hbm.1, bf16[64,64]{1,0:T(8,128)(2,1)} %fwd_middle_hbm.1, bf16[64,64]{1,0:T(8,128)(2,1)} %fwd_outer_hbm.1, ...), custom_call_target="tpu_custom_call" | custom-call | tf_op jit(solution)/shard_map/pallas_call | solution.py:655
  108.1 3.8 %copy.17 = bf16[2048,768]{1,0:T(8,128)(2,1)} copy(bf16[2048,768]{1,0:T(8,128)(2,1)} %shard_map.145) | data formatting | bytes 6291456

commit v3 on v2

--- a/solution.py
+++ b/solution.py
@@ -14,6 +14,7 @@
 NXY = 8
 NX = 4
 ROWS = 512
+HAND = 256
 BAND = 512
 
 
@@ -81,8 +82,8 @@
     total,
     staged,
     small_sem,
+    signal_sem,
     load_sem,
-    local_sem,
     core_send,
     core_recv,
     z_send,
@@ -149,22 +150,29 @@
         pltpu.make_async_copy(ref, twiddles.at[n], small_sem.at[6 + n])
         for n, ref in enumerate(given_tw)
     ]
+    def signal_load(i, n):
+        at = pl.ds(pl.multiple_of(n * ROWS, ROWS), ROWS)
+        return pltpu.make_async_copy(
+            signal.at[at, pl.ds(i * LANES, LANES)], sig.at[i, at], signal_sem.at[i, n]
+        )
+
+    for n in range(4):
+        signal_load(0, n).start()
     factor_loads[0].start()
     tw_loads[0].start()
     loads = []
     for i in range(nch):
         cols = pl.ds(i * LANES, LANES)
-        trio = (
-            pltpu.make_async_copy(signal.at[:, cols], sig.at[i], load_sem.at[0, i]),
-            pltpu.make_async_copy(spectral.at[:, :, :, cols], ker.at[i], load_sem.at[1, i]),
-            pltpu.make_async_copy(gate.at[:, cols], gat.at[i], load_sem.at[2, i]),
+        pair_of_loads = (
+            pltpu.make_async_copy(spectral.at[:, :, :, cols], ker.at[i], load_sem.at[0, i]),
+            pltpu.make_async_copy(gate.at[:, cols], gat.at[i], load_sem.at[1, i]),
         )
-        loads.append(trio)
-    loads[0][0].start()
+        loads.append(pair_of_loads)
     for copy in factor_loads[1:] + tw_loads[1:]:
         copy.start()
     for i in range(1, nch):
-        loads[i][0].start()
+        for n in range(4):
+            signal_load(i, n).start()
 
     barrier = pltpu.get_barrier_semaphore()
     pl.semaphore_signal(barrier, inc=1, device_id=twin, device_id_type=MESH)
@@ -224,9 +232,8 @@
     lax.fori_loop(0, 4, tw_in_body, 0)
 
     def stage_inner(i):
-        loads[i][0].wait()
-
         def body(n, carry):
+            signal_load(i, n).wait()
             base = pl.multiple_of(n * 512, 512)
             wide = jnp.concatenate(
                 [sig[i, pl.ds(base, 256), :], sig[i, pl.ds(base + 256, 256), :]], axis=1
@@ -256,7 +263,7 @@
     core_copies = [core_copy(i) for i in range(nch)]
     core_copies[0].start()
     for i in range(nch):
-        loads[i][1].start()
+        loads[i][0].start()
     stage_inner(1)
     core_copies[1].start()
     expand(fwd_middle, mat_m, in_z_order, lambda s: s)
@@ -304,14 +311,11 @@
             )
             copy.start()
             z_copies[i].append(copy)
-        own = pltpu.make_async_copy(send_z.at[i, z], recv_z.at[i, z], local_sem.at[0, i])
-        own.start()
-        z_copies[i].append(own)
+        recv_z[i, z] = send_z[i, z]
 
     def start_xy(i):
-        for copy in z_copies[i][:-1]:
+        for copy in z_copies[i]:
             copy.wait_recv()
-        z_copies[i][-1].wait()
         xy_copies[i] = []
         for e in order_xy:
             other, device = at_xy(e)
@@ -324,15 +328,12 @@
             )
             copy.start()
             xy_copies[i].append(copy)
-        own = pltpu.make_async_copy(recv_z.at[i, :, yx], recv_xy.at[i, yx], local_sem.at[1, i])
-        own.start()
-        xy_copies[i].append(own)
+        recv_xy[i, yx] = recv_z[i, :, yx]
 
     def stage_outer(i):
-        for copy in xy_copies[i][:-1]:
+        for copy in xy_copies[i]:
             copy.wait_recv()
-        xy_copies[i][-1].wait()
-        loads[i][1].wait()
+        loads[i][0].wait()
 
         def product(n, base, res):
             factor = ker[i, pl.ds(n * 32, 32)]
@@ -365,14 +366,11 @@
             )
             copy.start()
             xy2_copies[i].append(copy)
-        own = pltpu.make_async_copy(send_xy2.at[i, yx], recv_xy2.at[i, yx], local_sem.at[2, i])
-        own.start()
-        xy2_copies[i].append(own)
+        recv_xy2[i, yx] = send_xy2[i, yx]
 
     def start_z2(i):
-        for copy in xy2_copies[i][:-1]:
+        for copy in xy2_copies[i]:
             copy.wait_recv()
-        xy2_copies[i][-1].wait()
         z2_copies[i] = []
         for d in order_z:
             other, device = at_z(d)
@@ -385,9 +383,7 @@
             )
             copy.start()
             z2_copies[i].append(copy)
-        own = pltpu.make_async_copy(recv_xy2.at[i, :, z], recv_z2.at[i, z], local_sem.at[3, i])
-        own.start()
-        z2_copies[i].append(own)
+        recv_z2[i, z] = recv_xy2[i, :, z]
 
     def core2_copy(i):
         return remote(
@@ -397,9 +393,8 @@
     core2_copies = [core2_copy(i) for i in range(nch)]
 
     def stage_inv_middle(i):
-        for copy in z2_copies[i][:-1]:
+        for copy in z2_copies[i]:
             copy.wait_recv()
-        z2_copies[i][-1].wait()
 
         wide = pair(recv_z2, i)
 
@@ -471,7 +466,7 @@
         lax.fori_loop(0, sig.shape[1] // ROWS, body, 0)
 
     def make_silu(i):
-        loads[i][2].wait()
+        loads[i][1].wait()
 
         def body(n, carry):
             at = pl.ds(pl.multiple_of(n * 256, 256), 256)
@@ -536,7 +531,7 @@
     )
     w_own.start()
     for i in range(nch):
-        loads[i][2].start()
+        loads[i][1].start()
     stage_middle(1)
     stage_middle(2)
     expand(fwd_outer, mat_f, lambda q: q, lambda s: s)
@@ -566,9 +561,9 @@
     w_own.wait()
     stage_inv_middle(1)
     stage_inv_inner(1)
-    project(0, ((act, 0), (act, 1)))
     stage_inv_middle(2)
     stage_inv_inner(2)
+    project(0, ((act, 0), (act, 1)))
     w_copy.wait_recv()
     project(1, ((act, 2), (act_in, 0)))
     project(2, ((act_in, 1), (act_in, 2)))
@@ -577,13 +572,32 @@
         core_copies[i].wait_send()
         core2_copies[i].wait_send()
         for table in (z_copies, xy_copies, xy2_copies, z2_copies):
-            for copy in table[i][:-1]:
+            for copy in table[i]:
                 copy.wait_send()
         for n in range(sig.shape[1] // ROWS):
             act_copy(i, n).wait_send()
     w_copy.wait_send()
     for n in range(sig.shape[1] // ROWS):
         out_copy(n).wait()
+
+
+def hand_on(source, out, held, read_sem, write_sem):
+    blocks = [pl.ds(n * HAND, HAND) for n in range(source.shape[0] // HAND)]
+    reads = [
+        pltpu.make_async_copy(source.at[at], held.at[at], read_sem.at[n])
+        for n, at in enumerate(blocks)
+    ]
+    writes = [
+        pltpu.make_async_copy(held.at[at], out.at[at], write_sem.at[n])
+        for n, at in enumerate(blocks)
+    ]
+    for copy in reads:
+        copy.start()
+    for read, write in zip(reads, writes):
+        read.wait()
+        write.start()
+    for copy in writes:
+        copy.wait()
 
 
 def on_device(*args):
@@ -632,8 +646,8 @@
         pltpu.VMEM((tokens, width), F32),
         pltpu.VMEM((tokens, width), BF16),
         dma((11,)),
-        dma((3, nch)),
-        dma((4, nch)),
+        dma((nch, tokens // ROWS)),
+        dma((2, nch)),
         dma((nch,)),
         dma((nch,)),
         dma((nch, NZ)),
@@ -652,7 +666,7 @@
         dma(()),
         dma((tokens // ROWS,)),
     ]
-    return pl.pallas_call(
+    mixed = pl.pallas_call(
         kernel,
         out_shape=jax.ShapeDtypeStruct((tokens, width), BF16),
         in_specs=specs,
@@ -662,6 +676,18 @@
             collective_id=0, has_side_effects=True, vmem_limit_bytes=56 * 2**20
         ),
     )(*args)
+    return pl.pallas_call(
+        hand_on,
+        out_shape=jax.ShapeDtypeStruct((tokens, width), BF16),
+        in_specs=[big],
+        out_specs=big,
+        scratch_shapes=[
+            pltpu.VMEM((tokens, width), BF16),
+            dma((tokens // HAND,)),
+            dma((tokens // HAND,)),
+        ],
+        compiler_params=pltpu.CompilerParams(vmem_limit_bytes=60 * 2**20),
+    )(mixed)
 
 
 def solution(mesh):

time: 112 us -> 111 us (level)
  local copies, waits for them, and re-layouts: 3.76 us -> 0 us
  Pallas kernels: 108 us -> 111 us
    unnamed x1 -> x0, local copies, waits for them, and re-layouts: 3.76 us -> none
    pallas_call x0 -> x1, Pallas kernels: none -> 2.79 us  [on_device(): pl.pallas_call(hand_on, out_shape=jax.ShapeDtypeStruct((tokens, width), B...]
where the time goes in v3:
time: 111 us
  Pallas kernels  111 us (100%)
    pallas_call x1, Pallas kernels, on_device(): pl.pallas_call(kernel, out_shape=jax.ShapeDtypeStruct((tokens, width), BF...  108 us
    pallas_call x1, Pallas kernels, on_device(): pl.pallas_call(hand_on, out_shape=jax.ShapeDtypeStruct((tokens, width), B...  2.79 us

profile of v3, /device:TPU:1, one launch (start us, length us, event | category | flops | bytes accessed | tf_op | source)
XLA Modules:
  0.0 110.7 jit_solution(9547681246556231775)
XLA Ops:
  0.0 107.9 %shard_map.145.source = bf16[2048,768]{1,0:T(8,128)(2,1)} custom-call(bf16[2048,384]{1,0:T(8,128)(2,1)} %signal.1, bf16[2048,384]{1,0:T(8,128)(2,1)} %gate.1, bf16[64,2,16,384]{3,2,1,0:T(8,128)(2,1)} %spectral.1, bf16[64,64]{1,0:T(8,128)(2,1)} %fwd_inner_hbm.1, bf16[64,64]{1,0:T(8,128)(2,1)} %fwd_middle_hbm.1, bf16[64,64]{1,0:T(8,128)(2,1)} %fwd_outer_hbm.1, ...), custom_call_target="tpu_custom_call" | custom-call | tf_op jit(solution)/shard_map/pallas_call | solution.py:669
  107.9 2.8 %shard_map.146 = bf16[2048,768]{1,0:T(8,128)(2,1)} custom-call(bf16[2048,768]{1,0:T(8,128)(2,1)} %shard_map.145.source), custom_call_target="tpu_custom_call" | custom-call | tf_op jit(solution)/shard_map/pallas_call | solution.py:679

commit v4 on v3

--- a/solution.py
+++ b/solution.py
@@ -385,12 +385,15 @@
             z2_copies[i].append(copy)
         recv_z2[i, z] = recv_xy2[i, :, z]
 
-    def core2_copy(i):
+    def core2_copy(i, h):
+        at = pl.ds(h * 16, 16)
         return remote(
-            send_j.at[i], rows_j.at[i, :, core], core2_send.at[i], core2_recv.at[i], twin
+            send_j.at[i, at],
+            rows_j.at[i, at, core],
+            core2_send.at[i, h],
+            core2_recv.at[i, h],
+            twin,
         )
-
-    core2_copies = [core2_copy(i) for i in range(nch)]
 
     def stage_inv_middle(i):
         for copy in z2_copies[i]:
@@ -411,8 +414,9 @@
         def to_own(n, p, part):
             rows_j[i, pl.ds(n * 16, 16), core, p] = part
 
-        lax.fori_loop(2, 4, lambda n, c: (block(n, to_twin), c)[1], 0)
-        core2_copies[i].start()
+        for h in range(2):
+            block(2 + h, to_twin)
+            core2_copy(i, h).start()
         lax.fori_loop(0, 2, lambda n, c: (block(n, to_own), c)[1], 0)
 
     def act_copy(i, n):
@@ -422,7 +426,6 @@
         )
 
     def stage_inv_inner(i):
-        core2_copies[i].wait_recv()
         scale = skip[pl.ds(i * LANES, LANES)].reshape(1, LANES)
 
         def body(n, carry):
@@ -438,7 +441,9 @@
             act_copy(i, n).start()
             return carry
 
-        lax.fori_loop(0, 4, body, 0)
+        for h in range(2):
+            core2_copy(i, h).wait_recv()
+            lax.fori_loop(2 * h, 2 * h + 2, body, 0)
 
     def out_copy(n):
         at = pl.ds(pl.multiple_of(n * ROWS, ROWS), ROWS)
@@ -570,7 +575,8 @@
 
     for i in range(nch):
         core_copies[i].wait_send()
-        core2_copies[i].wait_send()
+        for h in range(2):
+            core2_copy(i, h).wait_send()
         for table in (z_copies, xy_copies, xy2_copies, z2_copies):
             for copy in table[i]:
                 copy.wait_send()
@@ -658,8 +664,8 @@
         dma((nch, NXY)),
         dma((nch, NZ)),
         dma((nch, NZ)),
-        dma((nch,)),
-        dma((nch,)),
+        dma((nch, 2)),
+        dma((nch, 2)),
         dma((nch, tokens // ROWS)),
         dma((nch, tokens // ROWS)),
         dma(()),

time: 111 us -> 111 us (level)
  no operation moved by 1% of the time
where the time goes in v4:
time: 111 us
  Pallas kernels  111 us (100%)
    pallas_call x1, Pallas kernels, on_device(): pl.pallas_call(kernel, out_shape=jax.ShapeDtypeStruct((tokens, width), BF...  108 us
    pallas_call x1, Pallas kernels, on_device(): pl.pallas_call(hand_on, out_shape=jax.ShapeDtypeStruct((tokens, width), B...  2.79 us

profile of v4, /device:TPU:1, one launch (start us, length us, event | category | flops | bytes accessed | tf_op | source)
XLA Modules:
  0.0 110.6 jit_solution(6738384780930853277)
XLA Ops:
  0.0 107.8 %shard_map.145.source = bf16[2048,768]{1,0:T(8,128)(2,1)} custom-call(bf16[2048,384]{1,0:T(8,128)(2,1)} %signal.1, bf16[2048,384]{1,0:T(8,128)(2,1)} %gate.1, bf16[64,2,16,384]{3,2,1,0:T(8,128)(2,1)} %spectral.1, bf16[64,64]{1,0:T(8,128)(2,1)} %fwd_inner_hbm.1, bf16[64,64]{1,0:T(8,128)(2,1)} %fwd_middle_hbm.1, bf16[64,64]{1,0:T(8,128)(2,1)} %fwd_outer_hbm.1, ...), custom_call_target="tpu_custom_call" | custom-call | tf_op jit(solution)/shard_map/pallas_call | solution.py:675
  107.8 2.8 %shard_map.146 = bf16[2048,768]{1,0:T(8,128)(2,1)} custom-call(bf16[2048,768]{1,0:T(8,128)(2,1)} %shard_map.145.source), custom_call_target="tpu_custom_call" | custom-call | tf_op jit(solution)/shard_map/pallas_call | solution.py:685
